TPU v7x, 32 devices: a whole 2x2x4 slice. The times are simulated.
32 devices in a mesh: section: 4 (over y, x), dp: 8 (over z, core).
Axes of the slice: x: 2, y: 2, z: 4, core: 2. Of those that a mesh axis runs over, the one named last changes fastest.
Arguments:
- hidden: bfloat16 [8, 256, 8192], P('dp', 'section'), may hold values from -1500 to 1500
- head: bfloat16 [16384, 8192], P('section', 'dp'), may hold values from -0.0625 to 0.0625
- block_id: int32 [8, 4], P(None, 'section'), may hold values from 0 to 7
- block_live: int32 [8, 4], P(None, 'section'), may hold values from 0 to 1, as said below
- teacher: bfloat16 [8, 256, 2048], P('dp', None, 'section'), may hold values from -400 to 400
Outputs:
- grad_hidden: bfloat16 [8, 256, 8192], P('dp', 'section')
- grad_head: bfloat16 [16384, 8192], P('section', 'dp')
Inputs may be any that keep to these rules, and one draw needn't show every extreme that they name: `block_live`: every micro-batch has at least one live section.
All inputs are finite; a program needn't handle non-finite values.
Results may differ from a plain program's by a relative error of at most 0.0056.
Values may be sent and summed in bfloat16 or wider, within the bound.
A program may use at most 128 MiB of HBM per device.

v0:
```python
import jax
import jax.numpy as jnp
from jax import lax
from jax.sharding import PartitionSpec as P

neg_fill = -1e30


def local(hidden, head, block_id, block_live, teacher):
    my_replica = lax.axis_index("dp")
    tok_local = hidden.shape[1]
    model_width = hidden.shape[2]
    block_rows = teacher.shape[2]
    col_width = head.shape[1]
    blocks = head.shape[0] // block_rows
    table = head.reshape(blocks, block_rows, col_width)
    block_ids = block_id[:, 0]
    live_flags = block_live[:, 0]
    picked = jnp.take(table, block_ids, axis=0)
    whole = lax.all_gather(hidden, "section", axis=1, tiled=True)
    hidden_rows = whole[0]
    own_live = lax.dynamic_index_in_dim(live_flags, my_replica, 0, keepdims=False) > 0
    full_rows = lax.all_to_all(picked, "dp", split_axis=0, concat_axis=2, tiled=True)[0]
    logits = jnp.einsum("td,rd->tr", hidden_rows, full_rows, preferred_element_type=jnp.float32)
    teach = teacher[0].astype(jnp.float32)
    live_value = jnp.where(own_live, 1.0, 0.0).astype(jnp.float32)
    stud_local = jnp.where(own_live, jnp.max(logits, axis=1), neg_fill)
    teach_local = jnp.where(own_live, jnp.max(teach, axis=1), neg_fill)
    stud_top, teach_top = lax.pmax((stud_local, teach_local), "section")
    stud_part = jnp.where(own_live, jnp.sum(jnp.exp(logits - stud_top[:, None]), axis=1), 0.0)
    teach_part = jnp.where(own_live, jnp.sum(jnp.exp(teach - teach_top[:, None]), axis=1), 0.0)
    stud_total, teach_total, live_count = lax.psum((stud_part, teach_part, live_value), "section")
    student = jnp.where(own_live, jnp.exp(logits - stud_top[:, None]) / stud_total[:, None], 0.0)
    teach_prob = jnp.where(
        own_live, jnp.exp(teach - teach_top[:, None]) / teach_total[:, None], 0.0
    )
    logit_grad = (block_rows * live_count * (student - teach_prob)).astype(jnp.bfloat16)
    summed = lax.psum_scatter(
        jnp.dot(logit_grad, full_rows, preferred_element_type=jnp.float32),
        "section",
        scatter_dimension=0,
        tiled=True,
    )
    grad_hidden = summed.astype(jnp.bfloat16).reshape(1, tok_local, model_width)
    contrib = jnp.einsum(
        "tr,td->rd", logit_grad, hidden_rows, preferred_element_type=jnp.float32
    ).astype(jnp.bfloat16)
    returned = lax.all_to_all(contrib[None], "dp", split_axis=2, concat_axis=0, tiled=True)
    block_range = jnp.arange(blocks, dtype=jnp.int32)[None, :]
    selector = jnp.where(
        (live_flags[:, None] > 0) & (block_ids[:, None] == block_range), 1.0, 0.0
    ).astype(jnp.bfloat16)
    grad_head = jnp.einsum("mb,mrc->brc", selector, returned, preferred_element_type=jnp.float32)
    grad_head = grad_head.astype(jnp.bfloat16).reshape(blocks * block_rows, col_width)
    return (grad_hidden, grad_head)


def solution(mesh):
    placed = (
        P("dp", "section", None),
        P("section", "dp"),
        P(None, "section"),
        P(None, "section"),
        P("dp", None, "section"),
    )
    return jax.shard_map(
        local,
        mesh=mesh,
        in_specs=placed,
        out_specs=(P("dp", "section", None), P("section", "dp")),
        check_vma=False,
    )
```

profile of v0, /device:TPU:0, one launch (start us, length us, event | category | flops | bytes accessed | tf_op | source)
XLA Modules:
  0.0 631.1 jit_solution(14182784534861804643)
XLA Ops:
  7.2 0.7 fusion.26
  7.8 0.7 and_bitcast_fusion
  8.5 8.2 %gather_fusion = bf16[8,512,1024]{2,1,0:T(8,128)(2,1)} fusion(bf16[8,512,1024]{2,1,0:T(8,128)(2,1)} %bitcast.57, s32[1024]{0:T(1024)S(1)} %pad_clamp_fusion), kind=kCustom, calls=%fused_computation | custom fusion | bytes 16777248 | tf_op jit(solution)/shard_map/jit(_take)/gather | solution.py:19
  16.7 7.6 %broadcast_select_fusion = bf16[8,512,1024]{2,1,0:T(8,128)(2,1)} fusion(bf16[8,512,1024]{2,1,0:T(8,128)(2,1)} %gather_fusion, pred[8]{0:T(512)(128)(4,1)S(1)} %and_bitcast_fusion), kind=kLoop, calls=%fused_computation.5 | loop fusion | flops 4194304 | bytes 16777224 | tf_op jit(solution)/shard_map/jit(_take)/select_n | solution.py:19
  24.4 0.0 copy-start
  24.4 0.0 copy-start.2
  24.4 6.5 %all-to-all-start = ((bf16[8,512,1024]{2,1,0:T(8,128)(2,1)}), bf16[8,512,1024]{2,1,0:T(8,128)(2,1)}, u32[]{:S(2)}, u32[]{:S(2)}) async-start(bf16[8,512,1024]{2,1,0:T(8,128)(2,1)} %broadcast_select_fusion), calls=%async_computation | async-start | bytes 16777216 | tf_op jit(solution)/shard_map/all_to_all | solution.py:23
  30.8 0.0 all-gather.2.cloned.1.call-start
  30.9 0.7 all-gather.2.cloned.1.call-update
  31.6 0.0 reduce-scatter.2.cloned.1.call-start
  31.6 0.0 copy-done
  31.6 0.1 copy.14
  31.8 0.1 reduce_max.24
  31.9 0.0 copy-done.2
  31.9 0.6 fusion.30
  33.1 181.7 %all-to-all-done = bf16[8,512,1024]{2,1,0:T(8,128)(2,1)} async-done(((bf16[8,512,1024]{2,1,0:T(8,128)(2,1)}), bf16[8,512,1024]{2,1,0:T(8,128)(2,1)}, u32[]{:S(2)}, u32[]{:S(2)}) %all-to-all-start) | async-done | bytes 8388640 | tf_op jit(solution)/shard_map/all_to_all | solution.py:23
  214.8 11.4 %copy.13 = bf16[1,512,8,1024]{1,3,2,0:T(8,128)(2,1)} copy(bf16[1,512,8,1024]{3,1,2,0:T(8,128)(2,1)} %bitcast.5) | data formatting | bytes 16777216 | tf_op jit(solution)/shard_map/all_to_all | solution.py:23
  226.2 0.0 all-gather.2.cloned.1.call-done
  226.2 7.0 %fusion.31 = (f32[256]{0:T(256)S(1)}, f32[512,256]{1,0:T(8,128)S(1)}) fusion(bf16[512,8192]{0,1:T(8,128)(2,1)} %bitcast.55, bf16[1,256,8192]{2,1,0:T(8,128)(2,1)} %all-gather.2.cloned.1.call-done), kind=kOutput, calls=%fused_computation.43 | convolution fusion | flops 2147614464 | bytes 13108224 | tf_op jit(solution)/shard_map/td,rd->tr/dot_general | solution.py:24
  233.2 0.7 convert_select_fusion
  233.8 9.9 %all-reduce.1 = (f32[256]{0:T(256)S(1)}, f32[256]{0:T(256)S(1)}) all-reduce(f32[256]{0:T(256)S(1)} %get-tuple-element.9, f32[256]{0:T(256)S(1)} %get-tuple-element.10), channel_id=1, replica_groups=mesh['section'=4,'dp'=8] {'section'}, use_global_device_ids=true, to_apply=%region_6.7 | all-reduce | flops 512 | bytes 4096 | tf_op jit(solution)/shard_map/pmax | solution.py:29
  243.7 0.1 fusion.11
  243.9 0.6 broadcast_select_fusion.1
  244.5 0.1 fusion.16
  244.7 0.6 broadcast_select_fusion.2
  245.3 8.7 %all-reduce = (f32[256]{0:T(256)S(1)}, f32[256]{0:T(256)S(1)}, f32[]{:T(128)}) all-reduce(f32[256]{0:T(256)S(1)} %broadcast_select_fusion.1, f32[256]{0:T(256)S(1)} %broadcast_select_fusion.2, f32[]{:T(128)S(6)} %select_n.61), channel_id=1, replica_groups=mesh['section'=4,'dp'=8] {'section'}, use_global_device_ids=true, to_apply=%region_8.9 | all-reduce | flops 513 | bytes 4104 | tf_op jit(solution)/shard_map/psum | solution.py:32
  254.7 9.8 %fusion.28 = f32[256,8192]{1,0:T(8,128)} fusion(bf16[512,8192]{0,1:T(8,128)(2,1)} %bitcast.56, f32[512,256]{1,0:T(8,128)S(1)} %get-tuple-element.8, bf16[1,256,512]{1,2,0:T(8,128)(2,1)S(1)} %copy.14, f32[256]{0:T(256)S(1)} %get-tuple-element.2, f32[256]{0:T(256)S(1)} %get-tuple-element.5, f32[256]{0:T(256)S(1)} %get-tuple-element.3, ...), kind=kOutput, calls=%fused_computation.41 | convolution fusion | flops 2148794368 | bytes 17567748 | tf_op jit(solution)/shard_map/dot_general | solution.py:39
  264.6 0.0 reduce-scatter.2.cloned.1.call-update
  264.6 8.7 %fusion = bf16[1,512,8192]{2,1,0:T(8,128)(2,1)} fusion(bf16[1,256,8192]{2,1,0:T(8,128)(2,1)} %all-gather.2.cloned.1.call-done, f32[512,256]{1,0:T(8,128)S(1)} %get-tuple-element.8, bf16[1,256,512]{1,2,0:T(8,128)(2,1)S(1)} %copy.14, f32[256]{0:T(256)S(1)} %get-tuple-element.2, f32[256]{0:T(256)S(1)} %get-tuple-element.5, f32[256]{0:T(256)S(1)} %get-tuple-element.3, ...), kind=kOutput, calls=%fused_computation.2 | convolution fusion | flops 2152988672 | bytes 13373445 | tf_op jit(solution)/shard_map/tr,td->rd/dot_general | solution.py:45
  273.3 35.0 %copy.15 = bf16[1,512,8192]{1,0,2:T(2,128)(2,1)} copy(bf16[1,512,8192]{2,1,0:T(8,128)(2,1)} %fusion) | data formatting | bytes 16777216 | tf_op jit(solution)/shard_map/broadcast_in_dim | solution.py:48
  308.3 0.5 broadcast.31
  308.8 54.8 %reduce.4 = bf16[8192,512]{1,0:T(8,128)(2,1)} reduce(bf16[8192,1,512]{2,1,0:T(2,128)(2,1)} %bitcast.53, bf16[]{:T(256)} %broadcast.31), dimensions={1}, to_apply=%bitcast.46.reduce_sub_computation | reduce | bytes 16777218
  363.6 11.2 %reshape.42 = bf16[8,2,262144]{2,1,0:T(2,128)(2,1)} reshape(bf16[8192,512]{1,0:T(8,128)(2,1)} %reduce.4) | data formatting | bytes 16777216
  374.8 5.3 all-to-all-start.1
  380.1 183.7 %all-to-all-done.1 = bf16[8,2,262144]{2,1,0:T(2,128)(2,1)} async-done(((bf16[8,2,262144]{2,1,0:T(2,128)(2,1)}), bf16[8,2,262144]{2,1,0:T(2,128)(2,1)}, u32[]{:S(2)}, u32[]{:S(2)}) %all-to-all-start.1) | async-done | bytes 8388640 | tf_op jit(solution)/shard_map/all_to_all | solution.py:48
  563.7 13.3 %reshape.43 = bf16[8192,1,512]{2,1,0:T(2,128)(2,1)} reshape(bf16[8,2,262144]{2,1,0:T(2,128)(2,1)} %all-to-all-done.1) | data formatting | bytes 16777216
  577.0 11.6 %copy.19 = bf16[1,512,8192]{1,2,0:T(8,128)(2,1)} copy(bf16[1,512,8192]{1,0,2:T(2,128)(2,1)} %bitcast.52) | data formatting | bytes 16777216
  588.6 0.0 copy-start.1
  588.6 12.6 %copy.18 = bf16[1,512,8,1024]{3,2,1,0:T(8,128)(2,1)} copy(bf16[1,512,8,1024]{1,3,2,0:T(8,128)(2,1)} %bitcast.54) | data formatting | bytes 16777216 | tf_op jit(solution)/shard_map/all_to_all | solution.py:48
  601.2 0.0 copy-done.1
  601.2 8.9 %fusion.3 = bf16[8,512,1024]{2,0,1:T(8,128)(2,1)} fusion(bf16[1,512,8,1024]{3,2,1,0:T(8,128)(2,1)} %copy.18, s32[8]{0:T(128)S(1)} %bitcast.59, pred[8]{0:T(512)(128)(4,1)S(1)} %compare_bitcast_fusion), kind=kOutput, calls=%fused_computation.6 | convolution fusion | flops 71303424 | bytes 16777256 | tf_op jit(solution)/shard_map/mb,mrc->brc/dot_general | solution.py:53
  610.1 11.5 %copy.17 = bf16[8,512,1024]{2,1,0:T(8,128)(2,1)} copy(bf16[8,512,1024]{2,0,1:T(8,128)(2,1)} %fusion.3) | data formatting | bytes 16777216 | tf_op jit(solution)/shard_map/convert_element_type | solution.py:54
  621.6 0.0 reduce-scatter.2.cloned.1.call-done
  621.6 2.7 convert_bitcast_fusion
  (2 shorter events, 0.0 us)
Async XLA Ops:
  24.4 7.2 %copy-start = (bf16[1,256,512]{2,1,0:T(8,128)(2,1)S(1)}, bf16[1,256,512]{2,1,0:T(8,128)(2,1)}, u32[]{:S(2)}) copy-start(bf16[1,256,512]{2,1,0:T(8,128)(2,1)} %param.9) | copy-start | bytes 786436
  24.4 7.5 %copy-start.2 = (s32[8,1]{0,1:T(1,128)S(1)}, s32[8,1]{0,1:T(1,128)}, u32[]{:S(2)}) copy-start(s32[8,1]{0,1:T(1,128)} %param.8) | copy-start | bytes 100
  24.4 190.5 %all-to-all-start = ((bf16[8,512,1024]{2,1,0:T(8,128)(2,1)}), bf16[8,512,1024]{2,1,0:T(8,128)(2,1)}, u32[]{:S(2)}, u32[]{:S(2)}) async-start(bf16[8,512,1024]{2,1,0:T(8,128)(2,1)} %broadcast_select_fusion), calls=%async_computation | async-start | bytes 16777216 | tf_op jit(solution)/shard_map/all_to_all | solution.py:23
  30.8 195.4 %all-gather.2.cloned.1.call-start = ((), (), s32[]{:S(2)}) async-start(), calls=%async_computation.3 | async-start | bytes 5242880 | tf_op jit(solution)/shard_map/all_gather | solution.py:20
  31.6 590.1 %reduce-scatter.2.cloned.1.call-start = ((), (), s32[]{:S(2)}) async-start(), calls=%async_computation.4 | async-start | bytes 10485760 | tf_op jit(solution)/shard_map/reduce_scatter | solution.py:38
  374.8 188.9 %all-to-all-start.1 = ((bf16[8,2,262144]{2,1,0:T(2,128)(2,1)}), bf16[8,2,262144]{2,1,0:T(2,128)(2,1)}, u32[]{:S(2)}, u32[]{:S(2)}) async-start(bf16[8,2,262144]{2,1,0:T(2,128)(2,1)} %reshape.42), calls=%async_computation.2 | async-start | bytes 16777216 | tf_op jit(solution)/shard_map/all_to_all | solution.py:48
  588.6 12.6 %copy-start.1 = (s32[8,1]{0,1:T(1,128)S(1)}, s32[8,1]{0,1:T(1,128)}, u32[]{:S(2)}) copy-start(s32[8,1]{0,1:T(1,128)} %param.7) | copy-start | bytes 100
Sparse Core Ops, SparseCore 0:
  33.5 54.1 all-gather.1
  264.7 84.3 reduce-scatter.1
where the time goes:
time: 634 us; the launch traced here: 631 us
  waiting for transfers between devices  366 us (58%)
  local copies, waits for them, and re-layouts  115 us (18%)
  other arithmetic  69.3 us (11%)
  matrix products  34.4 us (5%)
  blocking collectives  18.7 us (3%)
  between operations  15.5 us (2%)
  starting transfers between devices  11.8 us (2%)
    all_to_all x1, waiting for transfers between devices, local(): lax.all_to_all(contrib[None], 'dp', split_axis=2, concat_axis=0, tiled=True)  184 us
    all_to_all x1, waiting for transfers between devices, local(): lax.all_to_all(picked, 'dp', split_axis=0, concat_axis=2, tiled=True)[0]  182 us
    unnamed x1, other arithmetic  54.8 us
    unnamed x11, local copies, waits for them, and re-layouts  36.7 us
    broadcast_in_dim x1, local copies, waits for them, and re-layouts, local(): contrib[None]  35 us
  transfers between devices with their start and end apart: 4, of which 2 were waited for; matrix products, arithmetic and copies ran while one was open for 29% of the time, Pallas kernels for 0%

commit v1 on v0

v1 whole, which is shorter than its diff:
```python
import functools

import jax
import jax.numpy as jnp
from jax import lax
from jax.experimental import pallas as pl
from jax.experimental.pallas import tpu as pltpu
from jax.sharding import PartitionSpec as P

neg_fill = -1e30


def pick_body(ids, head_ref, out_ref):
    out_ref[0] = head_ref[...]


def pick_rows(block_ids, head, block_rows):
    width = head.shape[1]
    batches = block_ids.shape[0]
    return pl.pallas_call(
        pick_body,
        grid_spec=pltpu.PrefetchScalarGridSpec(
            num_scalar_prefetch=1,
            grid=(batches,),
            in_specs=[pl.BlockSpec((block_rows, width), lambda m, ids: (ids[m], 0))],
            out_specs=pl.BlockSpec((1, block_rows, width), lambda m, ids: (m, 0, 0)),
        ),
        out_shape=jax.ShapeDtypeStruct((batches, block_rows, width), head.dtype),
        cost_estimate=pl.CostEstimate(
            flops=0, bytes_accessed=4 * batches * block_rows * width, transcendentals=0
        ),
    )(block_ids, head)


def head_body(ids, live, grad_ref, hid_ref, out_ref, acc):
    block = pl.program_id(0)
    batches = grad_ref.shape[0]
    acc[...] = jnp.zeros_like(acc)

    def step(m, carry):
        @pl.when(jnp.logical_and(live[m] > 0, ids[m] == block))
        def _():
            term = lax.dot_general(
                grad_ref[m], hid_ref[m], (((0,), (0,)), ((), ())),
                preferred_element_type=jnp.float32,
            )
            acc[...] += term.astype(jnp.bfloat16).astype(jnp.float32)

        return carry

    lax.fori_loop(0, batches, step, 0)
    out_ref[...] = acc[...].astype(out_ref.dtype)


def head_grad(block_ids, live_flags, grad_all, hid_all, blocks):
    batches, tokens, block_rows = grad_all.shape
    width = hid_all.shape[2]
    return pl.pallas_call(
        head_body,
        grid_spec=pltpu.PrefetchScalarGridSpec(
            num_scalar_prefetch=2,
            grid=(blocks,),
            in_specs=[
                pl.BlockSpec(grad_all.shape, lambda b, ids, live: (0, 0, 0)),
                pl.BlockSpec(hid_all.shape, lambda b, ids, live: (0, 0, 0)),
            ],
            out_specs=pl.BlockSpec((block_rows, width), lambda b, ids, live: (b, 0)),
            scratch_shapes=[pltpu.VMEM((block_rows, width), jnp.float32)],
        ),
        out_shape=jax.ShapeDtypeStruct((blocks * block_rows, width), jnp.bfloat16),
        compiler_params=pltpu.CompilerParams(vmem_limit_bytes=48 * 2**20),
        cost_estimate=pl.CostEstimate(
            flops=2 * batches * tokens * block_rows * width,
            bytes_accessed=2 * (grad_all.size + hid_all.size + blocks * block_rows * width),
            transcendentals=0,
        ),
    )(block_ids, live_flags, grad_all, hid_all)


def local(hidden, head, block_id, block_live, teacher):
    my_replica = lax.axis_index("dp")
    block_rows = teacher.shape[2]
    blocks = head.shape[0] // block_rows
    block_ids = block_id[:, 0]
    live_flags = block_live[:, 0]
    picked = pick_rows(block_ids, head, block_rows)
    mine = lax.all_to_all(hidden, "dp", split_axis=2, concat_axis=0, tiled=True)
    hid_all = lax.all_gather(mine, "section", axis=1, tiled=True)
    own_live = lax.dynamic_index_in_dim(live_flags, my_replica, 0, keepdims=False) > 0
    partial = jnp.einsum("mtd,mrd->mtr", hid_all, picked, preferred_element_type=jnp.float32)
    logits = lax.psum_scatter(partial, "dp", scatter_dimension=0, tiled=True)[0]
    teach = teacher[0].astype(jnp.float32)
    live_value = jnp.where(own_live, 1.0, 0.0).astype(jnp.float32)
    stud_local = jnp.where(own_live, jnp.max(logits, axis=1), neg_fill)
    teach_local = jnp.where(own_live, jnp.max(teach, axis=1), neg_fill)
    stud_top, teach_top = lax.pmax((stud_local, teach_local), "section")
    stud_part = jnp.where(own_live, jnp.sum(jnp.exp(logits - stud_top[:, None]), axis=1), 0.0)
    teach_part = jnp.where(own_live, jnp.sum(jnp.exp(teach - teach_top[:, None]), axis=1), 0.0)
    stud_total, teach_total, live_count = lax.psum((stud_part, teach_part, live_value), "section")
    student = jnp.where(own_live, jnp.exp(logits - stud_top[:, None]) / stud_total[:, None], 0.0)
    teach_prob = jnp.where(
        own_live, jnp.exp(teach - teach_top[:, None]) / teach_total[:, None], 0.0
    )
    logit_grad = (block_rows * live_count * (student - teach_prob)).astype(jnp.bfloat16)
    grad_all = lax.all_gather(logit_grad, "dp", axis=0)
    terms = jnp.einsum("mtr,mrd->mtd", grad_all, picked, preferred_element_type=jnp.float32)
    summed = lax.psum_scatter(terms, "section", scatter_dimension=1, tiled=True)
    grad_hidden = lax.all_to_all(
        summed.astype(jnp.bfloat16), "dp", split_axis=0, concat_axis=2, tiled=True
    )
    grad_head = head_grad(block_ids, live_flags, grad_all, hid_all, blocks)
    return (grad_hidden, grad_head)


def solution(mesh):
    placed = (
        P("dp", "section", None),
        P("section", "dp"),
        P(None, "section"),
        P(None, "section"),
        P("dp", None, "section"),
    )
    return jax.shard_map(
        local,
        mesh=mesh,
        in_specs=placed,
        out_specs=(P("dp", "section", None), P("section", "dp")),
        check_vma=False,
    )
```

time: 634 us -> 406 us (0.64)
  waiting for transfers between devices: 366 us -> 217 us
  local copies, waits for them, and re-layouts: 115 us -> 22.6 us
  blocking collectives: 18.7 us -> 51 us
  Pallas kernels: 0 us -> 20.5 us
  matrix products: 34.4 us -> 18.5 us
  other arithmetic: 69.3 us -> 54.9 us
  starting transfers between devices: 11.8 us -> 4.95 us
    all_to_all x2 -> x1, waiting for transfers between devices: 365 us -> 15.9 us  [local(): lax.all_to_all(summed.astype(jnp.bfloat16), 'dp', split_axis=0, concat_ax...]
    reduce_scatter x1 -> x2, waiting for transfers between devices: 0.01 us -> 133 us  [the longest x1 86.1 us: local(): summed = lax.psum_scatter(terms, 'section', scatter_dimension=1, tiled=True)]
    all_gather x1 -> x2, waiting for transfers between devices: 0.01 us -> 68.2 us  [the longest x1 41.9 us: local(): hid_all = lax.all_gather(mine, 'section', axis=1, tiled=True)]
    broadcast_in_dim x1 -> x0, local copies, waits for them, and re-layouts: 35 us -> none  [local(): contrib[None]]
    all_to_all x0 -> x1, blocking collectives: none -> 32.7 us  [local(): mine = lax.all_to_all(hidden, 'dp', split_axis=2, concat_axis=0, tiled=True)]
    all_to_all x2, local copies, waits for them, and re-layouts: 24 us -> 2.68 us  [the longest x1 1.61 us: local(): mine = lax.all_to_all(hidden, 'dp', split_axis=2, concat_axis=0, tiled=True)]
    pallas_call x0 -> x2, Pallas kernels: none -> 20.5 us  [the longest x1 10.7 us: head_grad(): pl.pallas_call(head_body, grid_spec=pltpu.PrefetchScalarGridSpec(num_scal...]
    unnamed x11 -> x14, local copies, waits for them, and re-layouts: 36.7 us -> 19.1 us
  transfers between devices with their start and end apart: 4 -> 5, of which waited for: 2 -> 5; matrix products, arithmetic and copies ran while one was open for 29% -> 0% of each run, Pallas kernels for 0% -> 5%
where the time goes in v1:
time: 406 us; the launch traced here: 405 us
  waiting for transfers between devices  217 us (53%)
  other arithmetic  54.9 us (14%)
  blocking collectives  51 us (13%)
  local copies, waits for them, and re-layouts  22.6 us (6%)
  Pallas kernels  20.5 us (5%)
  matrix products  18.5 us (5%)
  between operations  15.1 us (4%)
  starting transfers between devices  4.95 us (1%)
    reduce_scatter x1, waiting for transfers between devices, local(): summed = lax.psum_scatter(terms, 'section', scatter_dimension=1, tiled=True)  86.1 us
    reduce_scatter x1, waiting for transfers between devices, local(): logits = lax.psum_scatter(partial, 'dp', scatter_dimension=0, tiled=True)[0]  47.1 us
    unnamed x1, other arithmetic  45.2 us
    all_gather x1, waiting for transfers between devices, local(): hid_all = lax.all_gather(mine, 'section', axis=1, tiled=True)  41.9 us
    all_to_all x1, blocking collectives, local(): mine = lax.all_to_all(hidden, 'dp', split_axis=2, concat_axis=0, tiled=True)  32.7 us
    all_gather x1, waiting for transfers between devices, local(): grad_all = lax.all_gather(logit_grad, 'dp', axis=0)  26.3 us
    unnamed x14, local copies, waits for them, and re-layouts  19.1 us
    all_to_all x1, waiting for transfers between devices, local(): lax.all_to_all(summed.astype(jnp.bfloat16), 'dp', split_axis=0, concat_ax...  15.9 us
  transfers between devices with their start and end apart: 5, of which 5 were waited for; matrix products, arithmetic and copies ran while one was open for 0% of the time, Pallas kernels for 5%

profile of v1, /device:TPU:0, one launch (start us, length us, event | category | flops | bytes accessed | tf_op | source)
XLA Modules:
  0.0 404.8 jit_solution(9634919216410733464)
XLA Ops:
  7.2 0.0 all-gather.6.cloned.1.call-start
  7.2 9.2 %copy.11 = bf16[1,64,8192]{1,0,2:T(2,128)(2,1)} copy(bf16[1,64,8192]{2,1,0:T(8,128)(2,1)} %param.5) | data formatting | bytes 2097152 | tf_op args[0]
  16.4 0.5 broadcast.17
  16.9 45.2 %reduce.3 = bf16[8192,64]{1,0:T(8,128)(2,1)S(1)} reduce(bf16[8192,1,64]{2,1,0:T(2,128)(2,1)} %bitcast.37, bf16[]{:T(256)} %broadcast.17), dimensions={1}, to_apply=%bitcast.29.reduce_sub_computation | reduce | bytes 2097154
  62.1 1.7 reshape.37
  63.8 32.7 %all_to_all.36 = bf16[8,2,32768]{2,1,0:T(2,128)(2,1)S(1)} all-to-all(bf16[8,2,32768]{2,1,0:T(2,128)(2,1)S(1)} %reshape.37), channel_id=1, replica_groups=mesh['section'=4,'dp'=8] {'dp'}, dimensions={0} | all-to-all | bytes 2097152 | tf_op jit(solution)/shard_map/all_to_all | solution.py:87
  96.5 4.2 %reshape.38 = bf16[8192,1,64]{2,1,0:T(2,128)(2,1)} reshape(bf16[8,2,32768]{2,1,0:T(2,128)(2,1)S(1)} %all_to_all.36) | data formatting | bytes 2097152
  100.8 2.5 copy.19
  103.2 1.6 copy.13
  104.9 0.0 all-gather.6.cloned.1.call-update
  104.9 0.0 reduce-scatter.3.cloned.1.call-start
  104.9 9.8 %shard_map.68 = bf16[8,512,1024]{2,1,0:T(8,128)(2,1)} custom-call(s32[8]{0:T(128)} %bitcast.34, bf16[4096,1024]{1,0:T(8,128)(2,1)} %head_ref.1), custom_call_target="tpu_custom_call" | custom-call | bytes 16777216 | tf_op jit(solution)/shard_map/pallas_call | solution.py:20
  114.7 41.9 %all-gather.6.cloned.1.call-done = bf16[8,1,256,1024]{3,2,0,1:T(8,128)(2,1)} async-done(((bf16[8,1,64,1024]{3,2,0,1:T(8,128)(2,1)}), bf16[8,1,256,1024]{3,2,0,1:T(8,128)(2,1)}) %all-gather.6.cloned.1.call-update) | async-done | bytes 4194320 | tf_op jit(solution)/shard_map/all_gather | solution.py:88
  156.7 8.9 %convolution_bitcast_fusion = f32[8,256,512]{1,2,0:T(8,128)} fusion(bf16[8,512,1024]{2,1,0:T(8,128)(2,1)} %shard_map.68, bf16[8,1,256,1024]{3,2,0,1:T(8,128)(2,1)} %all-gather.6.cloned.1.call-done), kind=kOutput, calls=%fused_computation | convolution fusion | flops 2147483648 | bytes 16777216 | tf_op jit(solution)/shard_map/mtd,mrd->mtr/dot_general | solution.py:90
  165.5 0.0 copy-start.3
  165.5 0.0 reduce-scatter.3.cloned.1.call-update
  165.5 0.0 all-gather.4.cloned.1.call-start
  165.6 0.9 copy-done.3
  166.5 0.1 copy.14
  166.6 0.1 reduce_max.24
  166.7 0.0 copy-done.2
  166.7 0.6 fusion.12
  168.0 0.6 convert_select_fusion
  168.6 47.1 %reduce-scatter.3.cloned.1.call-done = f32[1,256,512]{1,2,0:T(8,128)} async-done(((f32[8,256,512]{1,2,0:T(8,128)}), f32[1,256,512]{1,2,0:T(8,128)}) %reduce-scatter.3.cloned.1.call-update) | async-done | bytes 524304 | tf_op jit(solution)/shard_map/reduce_scatter | solution.py:91
  215.7 1.1 reduce_max.23
  216.8 0.6 broadcast_select_fusion.2
  217.5 9.9 %all-reduce.1 = (f32[256]{0:T(256)S(1)}, f32[256]{0:T(256)S(1)}) all-reduce(f32[256]{0:T(256)S(1)} %convert_select_fusion, f32[256]{0:T(256)S(1)} %broadcast_select_fusion.2), channel_id=1, replica_groups=mesh['section'=4,'dp'=8] {'section'}, use_global_device_ids=true, to_apply=%region_7.8 | all-reduce | flops 512 | bytes 4096 | tf_op jit(solution)/shard_map/pmax | solution.py:96
  227.3 0.1 fusion.7
  227.5 1.2 fusion.9
  228.6 0.6 broadcast_select_fusion
  229.3 8.4 %all-reduce = (f32[256]{0:T(256)S(1)}, f32[256]{0:T(256)S(1)}, f32[]{:T(128)}) all-reduce(f32[256]{0:T(256)S(1)} %get-tuple-element.7, f32[256]{0:T(256)S(1)} %get-tuple-element.8, f32[]{:T(128)S(6)} %select_n.43), channel_id=1, replica_groups=mesh['section'=4,'dp'=8] {'section'}, use_global_device_ids=true, to_apply=%region_9.10 | all-reduce | flops 513 | bytes 4104 | tf_op jit(solution)/shard_map/psum | solution.py:99
  238.3 1.9 fusion.10
  240.2 0.8 copy.15
  241.1 0.0 all-gather.4.cloned.1.call-update
  241.1 0.2 reduce-scatter.5.cloned.1.call-start
  241.3 26.3 %all-gather.4.cloned.1.call-done.grad_ref = bf16[8,256,512]{2,1,0:T(8,128)(2,1)} async-done(((bf16[1,256,512]{2,1,0:T(8,128)(2,1)}), bf16[8,256,512]{2,1,0:T(8,128)(2,1)}) %all-gather.4.cloned.1.call-update) | async-done | bytes 2097168 | tf_op jit(solution)/shard_map/all_gather | solution.py:105
  267.6 9.6 %fusion.13 = f32[8,256,1024]{2,1,0:T(8,128)} fusion(bf16[8,256,512]{2,1,0:T(8,128)(2,1)} %all-gather.4.cloned.1.call-done.grad_ref, bf16[8,512,1024]{2,1,0:T(8,128)(2,1)} %shard_map.68), kind=kOutput, calls=%fused_computation.22 | convolution fusion | flops 2147483648 | bytes 18874368 | tf_op jit(solution)/shard_map/mtr,mrd->mtd/dot_general | solution.py:106
  277.2 0.0 reduce-scatter.5.cloned.1.call-update
  277.3 0.0 copy-start
  277.3 0.0 copy-start.1
  277.3 86.1 %reduce-scatter.5.cloned.1.call-done = f32[8,64,1024]{2,1,0:T(8,128)} async-done(((f32[8,256,1024]{2,1,0:T(8,128)}), f32[8,64,1024]{2,1,0:T(8,128)}) %reduce-scatter.5.cloned.1.call-update) | async-done | bytes 2097168 | tf_op jit(solution)/shard_map/reduce_scatter | solution.py:107
  363.3 2.7 convert_element_type.20
  366.1 4.6 %all-to-all-start.1 = ((bf16[8,64,1024]{2,1,0:T(8,128)(2,1)}), bf16[8,64,1024]{2,1,0:T(8,128)(2,1)S(1)}, u32[]{:S(2)}, u32[]{:S(2)}) async-start(bf16[8,64,1024]{2,1,0:T(8,128)(2,1)} %convert_element_type.20), calls=%async_computation.3 | async-start | bytes 2097152 | tf_op jit(solution)/shard_map/all_to_all | solution.py:108
  370.7 0.0 copy-done
  370.7 0.0 copy-done.1
  370.7 10.7 %shard_map.69 = bf16[4096,1024]{1,0:T(8,128)(2,1)} custom-call(s32[8]{0:T(128)S(1)} %bitcast.35, s32[8]{0:T(128)S(1)} %bitcast.36, bf16[8,256,512]{2,1,0:T(8,128)(2,1)S(1)} %copy-done, bf16[8,256,1024]{2,1,0:T(8,128)(2,1)} %bitcast.42), custom_call_target="tpu_custom_call" | custom-call | flops 2147483648 | bytes 14680064 | tf_op jit(solution)/shard_map/pallas_call | solution.py:58
  381.4 15.9 %all-to-all-done.1 = bf16[8,64,1024]{2,1,0:T(8,128)(2,1)S(1)} async-done(((bf16[8,64,1024]{2,1,0:T(8,128)(2,1)}), bf16[8,64,1024]{2,1,0:T(8,128)(2,1)S(1)}, u32[]{:S(2)}, u32[]{:S(2)}) %all-to-all-start.1) | async-done | bytes 1048608 | tf_op jit(solution)/shard_map/all_to_all | solution.py:108
  397.3 1.1 copy.20
  (1 shorter events, 0.0 us)
Async XLA Ops:
  7.2 149.5 %all-gather.6.cloned.1.call-start = ((), (), s32[]{:S(2)}) async-start(), calls=%async_computation.7 | async-start | bytes 5242880 | tf_op jit(solution)/shard_map/all_gather | solution.py:88
  104.9 110.8 %reduce-scatter.3.cloned.1.call-start = ((), (), s32[]{:S(2)}) async-start(), calls=%async_computation.4 | async-start | bytes 4718592 | tf_op jit(solution)/shard_map/reduce_scatter | solution.py:91
  165.5 0.9 copy-start.3
  165.5 1.2 copy-start.2
  165.5 102.1 %all-gather.4.cloned.1.call-start = ((), (), s32[]{:S(2)}) async-start(), calls=%async_computation.5 | async-start | bytes 2359296 | tf_op jit(solution)/shard_map/all_gather | solution.py:105
  241.1 122.2 %reduce-scatter.5.cloned.1.call-start = ((), (), s32[]{:S(2)}) async-start(), calls=%async_computation.6 | async-start | bytes 10485760 | tf_op jit(solution)/shard_map/reduce_scatter | solution.py:107
  277.3 93.4 %copy-start = (bf16[8,256,512]{2,1,0:T(8,128)(2,1)S(1)}, bf16[8,256,512]{2,1,0:T(8,128)(2,1)}, u32[]{:S(2)}) copy-start(bf16[8,256,512]{2,1,0:T(8,128)(2,1)} %all-gather.4.cloned.1.call-done.grad_ref) | copy-start | bytes 6291460
  277.3 93.4 %copy-start.1 = (s32[8,1]{0,1:T(1,128)S(1)}, s32[8,1]{0,1:T(1,128)}, u32[]{:S(2)}) copy-start(s32[8,1]{0,1:T(1,128)} %param.7) | copy-start | bytes 100
  366.1 31.2 %all-to-all-start.1 = ((bf16[8,64,1024]{2,1,0:T(8,128)(2,1)}), bf16[8,64,1024]{2,1,0:T(8,128)(2,1)S(1)}, u32[]{:S(2)}, u32[]{:S(2)}) async-start(bf16[8,64,1024]{2,1,0:T(8,128)(2,1)} %convert_element_type.20), calls=%async_computation.3 | async-start | bytes 2097152 | tf_op jit(solution)/shard_map/all_to_all | solution.py:108
Sparse Core Ops, SparseCore 0:
  105.0 51.5 all-gather.5
  165.7 49.9 reduce-scatter.2
  241.2 26.3 all-gather.3
  277.4 85.9 reduce-scatter.4
